TPU v7x, 32 devices: a whole 2x2x4 slice. The times are simulated.
32 devices in a mesh: chan: 4 (over z), tm: 8 (over y, x, core).
Axes of the slice: x: 2, y: 2, z: 4, core: 2. Of those that a mesh axis runs over, the one named last changes fastest.
Arguments:
- raw_strain: float32 [256, 8192], P('chan', 'tm'), may hold values from -6 to 6
- whitening: float32 [1024], replicated, may hold values from -0.1875 to 0.1875
- block_mask: int32 [4, 4], replicated, may hold values from 0 to 1, as said below
- old_stack: float32 [32, 256, 256], P('tm', 'chan'), may hold values from -6 to 6
Outputs:
- new_stack: float32 [32, 256, 256], P('tm', 'chan')
Inputs may be any that keep to these rules, and one draw needn't show every extreme that they name: block_mask[a, b] is 1 exactly where (b - a) mod 4 is below a reach of row a, each reach at least 1, and 0 elsewhere.
All inputs are finite; a program needn't handle non-finite values.
Results may differ from a plain program's by a relative error of at most 0.0018.
Values may be sent and summed in bfloat16 or wider, within the bound.
A program may use at most 64 MiB of HBM per device.

v0:
```python
import jax
import jax.numpy as jnp
from jax import lax
from jax.sharding import PartitionSpec as P


def with_halo(block, sides, width):
    for axis, dim in sides:
        count = lax.axis_size(axis)
        forward = [(i, i + 1) for i in range(count - 1)]
        backward = [(target, source) for source, target in forward]
        low = lax.ppermute(
            lax.slice_in_dim(block, block.shape[dim] - width, None, axis=dim), axis, forward
        )
        high = lax.ppermute(lax.slice_in_dim(block, 0, width, axis=dim), axis, backward)
        block = jnp.concatenate([low, block, high], axis=dim)
    return block


def shifted_2(block, axis, distance):
    devices = range(lax.axis_size(axis))
    route = [(i - distance, i) for i in devices if i - distance in devices]
    return lax.ppermute(block, axis, route)


def passed_along(block, axis, distance):
    devices = range(lax.axis_size(axis))
    route = [((i - distance) % len(devices), i) for i in devices]
    return lax.ppermute(block, axis, route)


def toeplitz(whitening, out_count, window_len):
    period = window_len + 1
    taps_len = whitening.shape[0]
    padded_taps = jnp.concatenate([whitening, jnp.zeros((period - taps_len,), jnp.float32)])
    tiled = jnp.tile(padded_taps, out_count)[: out_count * window_len]
    return tiled.reshape(out_count, window_len)


def filter_blocks(padded, whitening, seg_len):
    taps_len = whitening.shape[0]
    channels = padded.shape[0]
    pieces = padded.reshape(channels, seg_len // taps_len + 1, taps_len)
    windows = jnp.concatenate([pieces[:, :-1], pieces[:, 1:]], axis=2)
    matrix = toeplitz(whitening, taps_len, 2 * taps_len)
    outputs = jnp.einsum("cbu,tu->cbt", windows, matrix, precision=lax.Precision.HIGHEST)
    return outputs.reshape(channels, seg_len)


def correlate(own_rows, partner, lag_count):
    seg_len = own_rows.shape[1]
    time_block = min(512, seg_len)

    def add_block(index, total):
        begin_at = index * time_block
        own_piece = lax.dynamic_slice_in_dim(own_rows, begin_at, time_block, 1)
        partner_slab = lax.dynamic_slice_in_dim(partner, begin_at, time_block + lag_count - 1, 1)
        shifted = jax.vmap(
            lambda offset: lax.dynamic_slice_in_dim(partner_slab, offset, time_block, 1)
        )(jnp.arange(lag_count, dtype=jnp.int32))
        return total + jnp.einsum(
            "it,ljt->lij", own_piece, shifted, preferred_element_type=jnp.float32
        )

    initial = jnp.zeros((lag_count, own_rows.shape[0], partner.shape[0]), jnp.float32)
    return lax.fori_loop(0, seg_len // time_block, add_block, initial)


def shards(raw_strain, whitening, block_mask, old_stack):
    channels, seg_len = raw_strain.shape
    taps_len = whitening.shape[0]
    lag_total = old_stack.shape[0] * lax.axis_size("tm")
    padded = with_halo(raw_strain, (("tm", 1),), taps_len // 2)
    filtered = filter_blocks(padded, whitening, seg_len).astype(jnp.bfloat16)
    leading = filtered[:, :lag_total]
    trailing = shifted_2(leading, "tm", -1)
    extended = jnp.concatenate([filtered, trailing], axis=1)
    cycle_size = lax.axis_size("chan")
    own_index = lax.axis_index("chan")
    total_channels = channels * cycle_size
    buffer = jnp.zeros((lag_total // lax.axis_size("tm"), channels, total_channels), jnp.float32)

    def visit_block(buffer, partner, position):
        paired = block_mask[own_index, position] > 0
        visit_part = lax.psum_scatter(
            lax.cond(
                paired,
                lambda: correlate(
                    filtered, partner, lag_total // lax.axis_size("tm") * lax.axis_size("tm")
                ),
                lambda: jnp.zeros(
                    (lag_total // lax.axis_size("tm") * lax.axis_size("tm"), channels, channels),
                    jnp.float32,
                ),
            ),
            "tm",
            scatter_dimension=0,
            tiled=True,
        )
        return lax.dynamic_update_slice_in_dim(buffer, visit_part, position * channels, 2)

    buffer = visit_block(buffer, extended, own_index)
    travel = extended
    for rounds in range(1, cycle_size):
        travel = passed_along(travel, "chan", 1)
        buffer = visit_block(buffer, travel, (own_index - rounds) % cycle_size)
    scaling = float(seg_len * lax.axis_size("tm")) ** (-0.5)
    return old_stack + buffer * scaling


def solution(mesh):
    in_specs = (P("chan", "tm"), P(), P(), P("tm", "chan", None))
    out_specs = P("tm", "chan", None)
    return jax.shard_map(shards, mesh=mesh, in_specs=in_specs, out_specs=out_specs, check_vma=False)
```

profile of v0, /device:TPU:0, one launch (start us, length us, event | category | flops | bytes accessed | tf_op | source)
XLA Modules:
  0.0 676.2 jit_solution(10649999411759759289)
XLA Ops:
  8.8 3.0 collective-permute-start
  12.6 4.0 tile.4
  16.6 13.3 %tile.10 = f32[2098176]{0:T(1024)} reshape(f32[1024,2049]{1,0:T(8,128)} %tile.4) | data formatting | bytes 16785408 | tf_op jit(solution)/shard_map/tile | solution.py:36
  29.9 5.8 slice.78
  35.6 9.3 %reshape.31 = f32[1024,2048]{1,0:T(8,128)} reshape(f32[2097152]{0:T(1024)} %slice.78) | data formatting | bytes 16777216 | tf_op jit(solution)/shard_map/reshape | solution.py:37
  46.3 10.4 %convolution_convert_fusion = bf16[64,1024]{1,0:T(8,128)(2,1)S(1)} fusion(f32[1024,2048]{1,0:T(8,128)} %reshape.31, f32[64,1,2048]{2,1,0:T(1,128)S(1)} %pad_maximum_fusion.1), kind=kOutput, calls=%fused_computation.32 | convolution fusion | flops 1610678272 | bytes 9043968 | tf_op jit(solution)/shard_map/cbu,tu->cbt/dot_general | solution.py:46
  59.4 2.5 collective-permute-done.2
  62.0 142.7 %conditional.4 = (f32[32,64,64]{1,2,0:T(8,128)}) conditional(s32[]{:T(128)} %bitcast, () %tuple.85, (bf16[64,1056]{1,0:T(8,128)(2,1)S(1)}, bf16[64,1024]{1,0:T(8,128)(2,1)S(1)}) %tuple.86), branch_computations={%region_0.0_spmd, %region_1.0_spmd} | conditional | flops 134479888 | bytes 3481807 | solution.py:86
  62.0 142.7 %while.66 = (s32[]{:T(128)}, f32[32,64,64]{1,2,0:T(8,128)}, bf16[64,1056]{1,0:T(8,128)(2,1)S(1)}, bf16[64,1024]{1,0:T(8,128)(2,1)S(1)}, s32[]{:T(128)}, /*index=...) while((s32[]{:T(128)}, f32[32,64,64]{1,2,0:T(8,128)}, ...), condition=%wide.region_3.0_spmd.clone, body=%wide.region_2.0_spmd.clone.sunk | while | flops 134479888 | bytes 3481703 | solution.py:66
  62.0 69.0 %while.79 = (s32[]{:T(128)}, bf16[64,543]{1,0:T(8,128)(2,1)S(1)}, bf16[32,64,512]{2,1,0:T(8,128)(2,1)S(1)}, s32[]{:T(128)}, s32[32,2]{1,0:T(8,128)}) while((s32[]{:T(128)}, bf16[64,543]{1,0:T(8,128)(2,1)S(1)}, bf16[32,64,512]{2,1,0:T(8,128)(2,1)S(1)}, s32[]{:T(128)}, s32[32,2]{1,0:T(8,128)}) %tuple.252), condition=%wide.while_cond.clone, body=%wide.while_body.sunk.clone.sunk | while | flops 2 | bytes 131177 | solution.py:59
  131.1 1.7 fusion.49
  132.8 69.0 %while.79 = (s32[]{:T(128)}, bf16[64,543]{1,0:T(8,128)(2,1)S(1)}, bf16[32,64,512]{2,1,0:T(8,128)(2,1)S(1)}, s32[]{:T(128)}, s32[32,2]{1,0:T(8,128)}) while((s32[]{:T(128)}, bf16[64,543]{1,0:T(8,128)(2,1)S(1)}, bf16[32,64,512]{2,1,0:T(8,128)(2,1)S(1)}, s32[]{:T(128)}, s32[32,2]{1,0:T(8,128)}) %tuple.252), condition=%wide.while_cond.clone, body=%wide.while_body.sunk.clone.sunk | while | flops 2 | bytes 131177 | solution.py:59
  201.8 2.9 fusion.49
  204.7 2.6 copy.9
  209.6 4.7 collective-permute-done.3
  215.4 2.5 copy.10
  218.7 133.7 %collective-permute-done.4 = bf16[64,1056]{1,0:T(8,128)(2,1)S(1)} collective-permute-done((bf16[64,1056]{1,0:T(8,128)(2,1)S(1)}, bf16[64,1056]{1,0:T(8,128)(2,1)S(1)}, u32[]{:S(2)}, u32[]{:S(2)}) %collective-permute-start.4) | collective-permute-done | bytes 135200 | tf_op jit(solution)/shard_map/ppermute | solution.py:29
  353.6 2.6 copy.11
  357.0 134.2 %collective-permute-done.5 = bf16[64,1056]{1,0:T(8,128)(2,1)S(1)} collective-permute-done((bf16[64,1056]{1,0:T(8,128)(2,1)S(1)}, bf16[64,1056]{1,0:T(8,128)(2,1)S(1)}, u32[]{:S(2)}, u32[]{:S(2)}) %collective-permute-start.5) | collective-permute-done | bytes 135200 | tf_op jit(solution)/shard_map/ppermute | solution.py:29
  492.4 2.6 copy.12
  496.4 1.8 dynamic_update_slice.13
  498.2 23.6 %reduce-scatter.9.cloned.1.call-done = f32[4,64,64]{2,1,0:T(8,128)} async-done(((f32[32,64,64]{2,1,0:T(8,128)}), f32[4,64,64]{2,1,0:T(8,128)}) %reduce-scatter.9.cloned.1.call-update) | async-done | bytes 65552 | tf_op jit(solution)/shard_map/reduce_scatter | solution.py:85
  522.9 144.2 %reduce-scatter.11.cloned.1.call-done = f32[4,64,64]{2,1,0:T(8,128)} async-done(((f32[32,64,64]{2,1,0:T(8,128)}), f32[4,64,64]{2,1,0:T(8,128)}) %reduce-scatter.11.cloned.1.call-update) | async-done | bytes 65552 | tf_op jit(solution)/shard_map/reduce_scatter | solution.py:85
  667.1 1.8 dynamic_update_slice.15
  (239 shorter events, 154.9 us)
Async XLA Ops:
  6.5 488.5 %reduce-scatter.5.cloned.1.call-start = ((), (), s32[]{:S(2)}) async-start(), calls=%async_computation.4 | async-start | bytes 1179648 | tf_op jit(solution)/shard_map/reduce_scatter | solution.py:85
  7.5 37.4 %collective-permute-start.1 = (f32[64,512]{1,0:T(8,128)S(1)}, f32[64,512]{1,0:T(8,128)S(1)}, u32[]{:S(2)}, u32[]{:S(2)}) collective-permute-start(f32[64,512]{1,0:T(8,128)S(1)} %get-tuple-element.560), channel_id=1, source_target_pairs={{1,0},{2,1},{3,2},{4,3},{5,4},{6,5},{7,6},{9,8},{10,9},{11,10},{12... | collective-permute-start | bytes 393224 | tf_op jit(solution)/shard_map/ppermute | solution.py:15
  8.8 36.1 %collective-permute-start = (f32[64,512]{1,0:T(8,128)S(1)}, f32[64,512]{1,0:T(8,128)S(1)}, u32[]{:S(2)}, u32[]{:S(2)}) collective-permute-start(f32[64,512]{1,0:T(8,128)S(1)} %get-tuple-element.559), channel_id=1, source_target_pairs={{0,1},{1,2},{2,3},{3,4},{4,5},{5,6},{6,7},{8,9},{9,10},{10,11},{11... | collective-permute-start | bytes 393224 | tf_op jit(solution)/shard_map/ppermute | solution.py:12
  35.6 9.3 %copy-start = (f32[64,1024]{1,0:T(8,128)S(1)}, f32[64,1024]{1,0:T(8,128)}, u32[]{:S(2)}) copy-start(f32[64,1024]{1,0:T(8,128)} %param.20) | copy-start | bytes 786436
  46.3 11.9 %copy-start.2 = (s32[4,4]{1,0:T(4,128)S(1)}, s32[4,4]{1,0:T(4,128)}, u32[]{:S(2)}) copy-start(s32[4,4]{1,0:T(4,128)} %param.22) | copy-start | bytes 196
  56.8 5.1 collective-permute-start.2
  207.3 289.1 %reduce-scatter.7.cloned.1.call-start = ((), (), s32[]{:S(2)}) async-start(), calls=%async_computation.5 | async-start | bytes 1179648 | tf_op jit(solution)/shard_map/reduce_scatter | solution.py:85
  207.3 7.0 %collective-permute-start.3 = (bf16[64,1056]{1,0:T(8,128)(2,1)S(1)}, bf16[64,1056]{1,0:T(8,128)(2,1)S(1)}, u32[]{:S(2)}, u32[]{:S(2)}) collective-permute-start(bf16[64,1056]{1,0:T(8,128)(2,1)S(1)} %pad_maximum_fusion.2), channel_id=1, source_target_pairs={{24,0},{0,8},{8,16},{16,24},{25,1},{1,9},{9,17},{17,25},{26,2},{2,... | collective-permute-start | bytes 405512 | tf_op jit(solution)/shard_map/ppermute | solution.py:29
  218.0 303.8 %reduce-scatter.9.cloned.1.call-start = ((), (), s32[]{:S(2)}) async-start(), calls=%async_computation.6 | async-start | bytes 1179648 | tf_op jit(solution)/shard_map/reduce_scatter | solution.py:85
  218.0 134.4 %collective-permute-start.4 = (bf16[64,1056]{1,0:T(8,128)(2,1)S(1)}, bf16[64,1056]{1,0:T(8,128)(2,1)S(1)}, u32[]{:S(2)}, u32[]{:S(2)}) collective-permute-start(bf16[64,1056]{1,0:T(8,128)(2,1)S(1)} %collective-permute-done.3), channel_id=1, source_target_pairs={{24,0},{0,8},{8,16},{16,24},{25,1},{1,9},{9,17},{17,25},{26,2},{2,... | collective-permute-start | bytes 405512 | tf_op jit(solution)/shard_map/ppermute | solution.py:29
  356.1 311.0 %reduce-scatter.11.cloned.1.call-start = ((), (), s32[]{:S(2)}) async-start(), calls=%async_computation.7 | async-start | bytes 1179648 | tf_op jit(solution)/shard_map/reduce_scatter | solution.py:85
  356.2 135.1 %collective-permute-start.5 = (bf16[64,1056]{1,0:T(8,128)(2,1)S(1)}, bf16[64,1056]{1,0:T(8,128)(2,1)S(1)}, u32[]{:S(2)}, u32[]{:S(2)}) collective-permute-start(bf16[64,1056]{1,0:T(8,128)(2,1)S(1)} %collective-permute-done.4), channel_id=1, source_target_pairs={{24,0},{0,8},{8,16},{16,24},{25,1},{1,9},{9,17},{17,25},{26,2},{2,... | collective-permute-start | bytes 405512 | tf_op jit(solution)/shard_map/ppermute | solution.py:29
  492.4 176.6 %copy-start.1 = (f32[4,64,256]{2,1,0:T(8,128)S(1)}, f32[4,64,256]{2,1,0:T(8,128)}, u32[]{:S(2)}) copy-start(f32[4,64,256]{2,1,0:T(8,128)} %param.23) | copy-start | bytes 786436
Sparse Core Ops, SparseCore 0:
  207.4 40.2 reduce-scatter.4
  250.9 133.4 reduce-scatter.6
  387.6 134.1 reduce-scatter.8
  524.8 142.2 reduce-scatter.10
where the time goes:
time: 687 us; the launch traced here: 676 us
  waiting for transfers between devices  443 us (64%)
  local copies, waits for them, and re-layouts  192 us (28%)
  between operations  15.9 us (2%)
  matrix products  15 us (2%)
  starting transfers between devices  7.64 us (1%)
    ppermute x3, waiting for transfers between devices, passed_along(): return lax.ppermute(block, axis, route)  273 us
    reduce_scatter x4, waiting for transfers between devices, visit_block(): lax.psum_scatter(lax.cond(paired, lambda: correlate(filtered, partner, la...  168 us
    gather x192, local copies, waits for them, and re-layouts  137 us
    another operation x2, local copies, waits for them, and re-layouts, toeplitz(): tiled = jnp.tile(padded_taps, out_count)[:out_count * window_len]  17.3 us
  transfers between devices with their start and end apart: 10, of which 6 were waited for; matrix products, arithmetic and copies ran while one was open for 7% of the time, Pallas kernels for 0%

commit v1 on v0

v1 whole, which is shorter than its diff:
```python
import functools

import jax
import jax.numpy as jnp
from jax import lax
from jax.experimental import pallas as pl
from jax.experimental.pallas import tpu as pltpu
from jax.sharding import PartitionSpec as P

MESH = pl.DeviceIdType.MESH
LANES = 128
NT = (((1,), (1,)), ((), ()))


def toeplitz_kernel(taps_ref, high_ref, both_ref):
    rows, width = high_ref.shape
    spread = jnp.broadcast_to(taps_ref[...], (rows, width))
    matrix = pltpu.roll(spread, 0, 1, stride=1, stride_axis=0)
    high = matrix.astype(jnp.bfloat16)
    low = (matrix - high.astype(jnp.float32)).astype(jnp.bfloat16)
    high_ref[...] = high
    both_ref[:rows] = high
    both_ref[rows:] = low


def toeplitz(whitening):
    width = whitening.shape[0] + LANES
    taps = jnp.pad(whitening, (0, LANES)).reshape(1, width)
    return pl.pallas_call(
        toeplitz_kernel,
        out_shape=(
            jax.ShapeDtypeStruct((LANES, width), jnp.bfloat16),
            jax.ShapeDtypeStruct((2 * LANES, width), jnp.bfloat16),
        ),
    )(taps)


def main_kernel(
    n_chan, n_tm, lag_total, half, left,
    raw_ref, high_ref, both_ref, out_ref,
    low_halo, high_halo, win_high, win_low, wide, stack, blocks, part, near, sent, far,
    halo_send, halo_recv, gather_send, gather_recv, near_send, near_recv, far_send, far_recv,
):
    chan, tm = lax.axis_index("chan"), lax.axis_index("tm")
    channels, seg = raw_ref.shape
    chips = n_tm // 2
    chip, core = tm // 2, lax.rem(tm, 2)
    lag_rows = channels * (lag_total // n_tm)

    barrier = pltpu.get_barrier_semaphore()
    for d in range(1, n_tm):
        pl.semaphore_signal(
            barrier, inc=1, device_id=(chan, lax.rem(tm + d, n_tm)), device_id_type=MESH
        )
    for d in range(1, n_chan):
        pl.semaphore_signal(
            barrier, inc=1, device_id=(lax.rem(chan + d, n_chan), tm), device_id_type=MESH
        )
    pl.semaphore_wait(barrier, n_tm - 1 + n_chan - 1)

    to_right = pltpu.make_async_remote_copy(
        src_ref=raw_ref.at[:, pl.ds(seg - half - left, half + left)],
        dst_ref=low_halo,
        send_sem=halo_send.at[0],
        recv_sem=halo_recv.at[0],
        device_id=(chan, lax.rem(tm + 1, n_tm)),
        device_id_type=MESH,
    )
    to_left = pltpu.make_async_remote_copy(
        src_ref=raw_ref.at[:, pl.ds(0, half)],
        dst_ref=high_halo,
        send_sem=halo_send.at[1],
        recv_sem=halo_recv.at[1],
        device_id=(chan, lax.rem(tm + n_tm - 1, n_tm)),
        device_id_type=MESH,
    )
    to_right.start()
    to_left.start()
    to_right.wait_recv()
    to_left.wait_recv()
    not_first = (tm > 0).astype(jnp.float32)
    not_last = (tm < n_tm - 1).astype(jnp.float32)
    padded = jnp.concatenate(
        [low_halo[...] * not_first, raw_ref[...], high_halo[...] * not_last], axis=1
    )
    high = padded.astype(jnp.bfloat16)
    low = (padded - high.astype(jnp.float32)).astype(jnp.bfloat16)
    pieces = (seg + left) // LANES
    width = 2 * half + LANES
    for b in range(pieces):
        win_high[pl.ds(b * channels, channels)] = high[:, b * LANES : b * LANES + width]
        win_low[pl.ds(b * channels, channels)] = low[:, b * LANES : b * LANES + width]
    both = lax.dot_general(
        win_high[...], both_ref[...], NT, preferred_element_type=jnp.float32
    )
    rest = lax.dot_general(
        win_low[...], high_ref[...], NT, preferred_element_type=jnp.float32
    )
    total = both[:, :LANES] + (both[:, LANES:] + rest)
    rounded = total.astype(jnp.bfloat16)
    ahead = left // LANES
    for b in range(ahead, pieces):
        blocks[chan, :, pl.ds((b - ahead) * LANES, LANES)] = rounded[
            b * channels : (b + 1) * channels
        ]

    gathers = []
    for d in range(1, n_chan):
        gathers.append(
            pltpu.make_async_remote_copy(
                src_ref=blocks.at[chan],
                dst_ref=blocks.at[chan],
                send_sem=gather_send.at[d],
                recv_sem=gather_recv.at[d],
                device_id=(lax.rem(chan + d, n_chan), tm),
                device_id_type=MESH,
            )
        )
        gathers[-1].start()

    exact = rounded.astype(jnp.float32)
    for b in range(pieces):
        piece = exact[b * channels : (b + 1) * channels]
        wide[:, pl.ds(b * LANES, LANES)] = piece * not_first if b < ahead else piece
    for lag in range(lag_total):
        q, row = divmod(lag * channels, lag_rows)
        moved = wide[...] if lag == 0 else pltpu.roll(wide[...], lag, 1)
        stack[q, pl.ds(row, channels)] = moved[:, left:].astype(jnp.bfloat16)
    for copy in gathers:
        copy.wait_recv()

    partner = blocks[...].reshape(n_chan * channels, seg)

    def partial_sums(q):
        return lax.dot_general(stack[q], partner, NT, preferred_element_type=jnp.float32)

    near_copies = []
    for d in range(chips):
        owner = lax.rem(chip + d + 1, chips)
        part[d] = partial_sums(owner * 2 + 1 - core)
        near_copies.append(
            pltpu.make_async_remote_copy(
                src_ref=part.at[d],
                dst_ref=near.at[d],
                send_sem=near_send.at[d],
                recv_sem=near_recv.at[d],
                device_id=(chan, chip * 2 + 1 - core),
                device_id_type=MESH,
            )
        )
        near_copies[-1].start()
    far_copies = []
    for d in range(chips - 1):
        owner = lax.rem(chip + d + 1, chips)
        own = partial_sums(owner * 2 + core)
        near_copies[d].wait_recv()
        sent[d] = (own + near[d]).astype(jnp.bfloat16)
        far_copies.append(
            pltpu.make_async_remote_copy(
                src_ref=sent.at[d],
                dst_ref=far.at[d],
                send_sem=far_send.at[d],
                recv_sem=far_recv.at[d],
                device_id=(chan, owner * 2 + core),
                device_id_type=MESH,
            )
        )
        far_copies[-1].start()
    own = partial_sums(chip * 2 + core)
    near_copies[chips - 1].wait_recv()
    own = own + near[chips - 1]
    for d in range(chips - 1):
        far_copies[d].wait_recv()
        own = own + far[d].astype(jnp.float32)
    out_ref[...] = own

    to_right.wait_send()
    to_left.wait_send()
    for copy in gathers + near_copies + far_copies:
        copy.wait_send()


def shards(n_chan, n_tm, raw_strain, whitening, block_mask, old_stack):
    channels, seg = raw_strain.shape
    taps = whitening.shape[0]
    half = taps // 2
    lags = old_stack.shape[0]
    lag_total = lags * n_tm
    left = -(-lag_total // LANES) * LANES
    chips = n_tm // 2
    rows = channels * lags
    every = n_chan * channels
    width = taps + LANES
    windows = channels * (seg + left) // LANES
    high, both = toeplitz(whitening)
    dma = pltpu.SemaphoreType.DMA
    sums = pl.pallas_call(
        functools.partial(main_kernel, n_chan, n_tm, lag_total, half, left),
        out_shape=jax.ShapeDtypeStruct((rows, every), jnp.float32),
        in_specs=[pl.BlockSpec(memory_space=pltpu.VMEM)] * 3,
        out_specs=pl.BlockSpec(memory_space=pltpu.VMEM),
        scratch_shapes=[
            pltpu.VMEM((channels, half + left), jnp.float32),
            pltpu.VMEM((channels, half), jnp.float32),
            pltpu.VMEM((windows, width), jnp.bfloat16),
            pltpu.VMEM((windows, width), jnp.bfloat16),
            pltpu.VMEM((channels, seg + left), jnp.float32),
            pltpu.VMEM((n_tm, rows, seg), jnp.bfloat16),
            pltpu.VMEM((n_chan, channels, seg), jnp.bfloat16),
            pltpu.VMEM((chips, rows, every), jnp.float32),
            pltpu.VMEM((chips, rows, every), jnp.float32),
            pltpu.VMEM((chips, rows, every), jnp.bfloat16),
            pltpu.VMEM((chips, rows, every), jnp.bfloat16),
            dma((2,)),
            dma((2,)),
            dma((n_chan,)),
            dma((n_chan,)),
            dma((chips,)),
            dma((chips,)),
            dma((chips,)),
            dma((chips,)),
        ],
        compiler_params=pltpu.CompilerParams(
            collective_id=0, has_side_effects=True, vmem_limit_bytes=40 * 1024 * 1024
        ),
    )(raw_strain, high, both)
    scaling = float(seg * n_tm) ** (-0.5)
    mask_row = lax.dynamic_index_in_dim(block_mask, lax.axis_index("chan"), 0, keepdims=False)
    weights = jnp.repeat(mask_row.astype(jnp.float32) * scaling, channels)
    return old_stack + sums.reshape(lags, channels, every) * weights


def solution(mesh):
    body = functools.partial(shards, mesh.shape["chan"], mesh.shape["tm"])
    in_specs = (P("chan", "tm"), P(), P(), P("tm", "chan", None))
    out_specs = P("tm", "chan", None)
    return jax.shard_map(body, mesh=mesh, in_specs=in_specs, out_specs=out_specs, check_vma=False)
```

time: 687 us -> 40.7 us (0.06); the launches traced: 676 us -> 40.4 us
  waiting for transfers between devices: 443 us -> 0 us
  local copies, waits for them, and re-layouts: 192 us -> 4.42 us
  Pallas kernels: 0 us -> 34.5 us
  between operations: 15.9 us -> 0.02 us
  matrix products: 15 us -> 0 us
  starting transfers between devices: 7.64 us -> 0 us
    ppermute x6 -> x0, waiting for transfers between devices: 275 us -> none  [the longest x3 273 us: passed_along(): return lax.ppermute(block, axis, route)]
    reduce_scatter x4 -> x0, waiting for transfers between devices: 168 us -> none  [visit_block(): lax.psum_scatter(lax.cond(paired, lambda: correlate(filtered, partner, la...]
    gather x192 -> x0, local copies, waits for them, and re-layouts: 137 us -> none
    pallas_call x0 -> x2, Pallas kernels: none -> 34.5 us  [the longest x1 32.7 us: shards(): pl.pallas_call(functools.partial(main_kernel, n_chan, n_tm, lag_total, ha...]
    another operation x5 -> x0, local copies, waits for them, and re-layouts: 20.6 us -> none  [the longest x2 17.3 us: toeplitz(): tiled = jnp.tile(padded_taps, out_count)[:out_count * window_len]]
    dot_general x3 -> x0, matrix products: 15 us -> none  [the longest x1 10.4 us: filter_blocks(): jnp.einsum('cbu,tu->cbt', windows, matrix, precision=lax.Precision.HIGHEST)]
    cond x4 -> x0, local copies, waits for them, and re-layouts: 10.2 us -> none  [visit_block(): lax.cond(paired, lambda: correlate(filtered, partner, lag_total // lax.ax...]
    reshape x2 -> x1, local copies, waits for them, and re-layouts: 9.74 us -> 0.6 us  [toeplitz(): taps = jnp.pad(whitening, (0, LANES)).reshape(1, width)]
  transfers between devices with their start and end apart: 10 -> 0, of which waited for: 6 -> 0; matrix products, arithmetic and copies ran while one was open for 7% -> 0% of each run, Pallas kernels for 0% -> 0%
where the time goes in v1:
time: 40.7 us; the launch traced here: 40.4 us
  Pallas kernels  34.5 us (85%)
  local copies, waits for them, and re-layouts  4.42 us (11%)
  other arithmetic  1.43 us (4%)
    pallas_call x1, Pallas kernels, shards(): pl.pallas_call(functools.partial(main_kernel, n_chan, n_tm, lag_total, ha...  32.7 us
    unnamed x8, local copies, waits for them, and re-layouts  2.98 us
    pallas_call x1, Pallas kernels, toeplitz(): pl.pallas_call(toeplitz_kernel, out_shape=(jax.ShapeDtypeStruct((LANES, w...  1.83 us

profile of v1, /device:TPU:0, one launch (start us, length us, event | category | flops | bytes accessed | tf_op | source)
XLA Modules:
  0.0 40.4 jit_solution(2494927567870243005)
XLA Ops:
  0.0 0.7 %pad.4 = f32[1152]{0:T(1024)S(1)} pad(f32[1024]{0:T(1024)} %param.5, f32[]{:T(128)} %constant.5.clone.1), padding=0_128 | pad | bytes 8708 | tf_op jit(solution)/shard_map/jit(_pad)/pad | solution.py:28
  0.7 0.6 %reshape.10.taps_ref = f32[1,1152]{1,0:T(1,128)} reshape(f32[1152]{0:T(1024)S(1)} %pad.4) | data formatting | bytes 9216 | tf_op jit(solution)/shard_map/reshape | solution.py:28
  1.3 1.8 %shard_map.46 = (bf16[128,1152]{1,0:T(8,128)(2,1)}, bf16[256,1152]{1,0:T(8,128)(2,1)}) custom-call(f32[1,1152]{1,0:T(1,128)} %reshape.10.taps_ref), custom_call_target="tpu_custom_call" | custom-call | tf_op jit(solution)/shard_map/pallas_call | solution.py:29
  3.1 0.0 copy-start
  3.1 1.1 %copy-done = bf16[256,1152]{1,0:T(8,128)(2,1)S(1)} copy-done((bf16[256,1152]{1,0:T(8,128)(2,1)S(1)}, bf16[256,1152]{1,0:T(8,128)(2,1)}, u32[]{:S(2)}) %copy-start) | copy-done | bytes 589848
  4.2 0.0 copy-start.1
  4.2 1.0 %copy-done.1 = bf16[128,1152]{1,0:T(8,128)(2,1)S(1)} copy-done((bf16[128,1152]{1,0:T(8,128)(2,1)S(1)}, bf16[128,1152]{1,0:T(8,128)(2,1)}, u32[]{:S(2)}) %copy-start.1) | copy-done | bytes 294936
  5.1 0.0 copy-start.2
  5.1 0.9 %copy-done.2 = f32[64,1024]{1,0:T(8,128)S(1)} copy-done((f32[64,1024]{1,0:T(8,128)S(1)}, f32[64,1024]{1,0:T(8,128)}, u32[]{:S(2)}) %copy-start.2) | copy-done | bytes 262168
  6.1 0.0 copy-start.3
  6.1 32.7 %shard_map.47 = f32[256,256]{1,0:T(8,128)S(1)} custom-call(f32[64,1024]{1,0:T(8,128)S(1)} %copy-done.2, bf16[128,1152]{1,0:T(8,128)(2,1)S(1)} %copy-done.1, bf16[256,1152]{1,0:T(8,128)(2,1)S(1)} %copy-done), custom_call_target="tpu_custom_call" | custom-call | tf_op jit(solution)/shard_map/pallas_call | solution.py:197
  38.8 0.7 %multiply_bitcast_fusion = f32[4]{0:T(128)S(1)} fusion(s32[4,4]{1,0:T(4,128)} %param.6, s32[]{:T(128)S(6)} %select_n.4), kind=kLoop, calls=%fused_computation.1 | loop fusion | flops 8 | bytes 36 | tf_op jit(solution)/shard_map/mul | solution.py:229
  39.5 0.1 broadcast_in_dim.3
  39.5 0.1 mul.18
  39.6 0.0 copy-done.3
  39.6 0.7 %multiply_add_fusion = f32[4,64,256]{2,1,0:T(8,128)} fusion(f32[4,64,256]{2,1,0:T(8,128)S(1)} %copy-done.3, f32[4,64,256]{2,1,0:T(8,128)S(1)} %bitcast.3, f32[256]{0:T(256)S(1)} %mul.18), kind=kLoop, calls=%fused_computation | loop fusion | flops 131072 | bytes 787456 | tf_op jit(solution)/shard_map/add | solution.py:230
Async XLA Ops:
  3.1 1.1 %copy-start = (bf16[256,1152]{1,0:T(8,128)(2,1)S(1)}, bf16[256,1152]{1,0:T(8,128)(2,1)}, u32[]{:S(2)}) copy-start(bf16[256,1152]{1,0:T(8,128)(2,1)} %get-tuple-element.8.both_ref) | copy-start | bytes 1769476
  4.2 1.0 %copy-start.1 = (bf16[128,1152]{1,0:T(8,128)(2,1)S(1)}, bf16[128,1152]{1,0:T(8,128)(2,1)}, u32[]{:S(2)}) copy-start(bf16[128,1152]{1,0:T(8,128)(2,1)} %get-tuple-element.7.high_ref) | copy-start | bytes 884740
  5.1 0.9 %copy-start.2 = (f32[64,1024]{1,0:T(8,128)S(1)}, f32[64,1024]{1,0:T(8,128)}, u32[]{:S(2)}) copy-start(f32[64,1024]{1,0:T(8,128)} %raw_ref.1) | copy-start | bytes 786436
  6.1 33.5 %copy-start.3 = (f32[4,64,256]{2,1,0:T(8,128)S(1)}, f32[4,64,256]{2,1,0:T(8,128)}, u32[]{:S(2)}) copy-start(f32[4,64,256]{2,1,0:T(8,128)} %param.7) | copy-start | bytes 786436

commit v2 on v1

--- a/solution.py
+++ b/solution.py
@@ -12,34 +12,11 @@
 NT = (((1,), (1,)), ((), ()))
 
 
-def toeplitz_kernel(taps_ref, high_ref, both_ref):
-    rows, width = high_ref.shape
-    spread = jnp.broadcast_to(taps_ref[...], (rows, width))
-    matrix = pltpu.roll(spread, 0, 1, stride=1, stride_axis=0)
-    high = matrix.astype(jnp.bfloat16)
-    low = (matrix - high.astype(jnp.float32)).astype(jnp.bfloat16)
-    high_ref[...] = high
-    both_ref[:rows] = high
-    both_ref[rows:] = low
-
-
-def toeplitz(whitening):
-    width = whitening.shape[0] + LANES
-    taps = jnp.pad(whitening, (0, LANES)).reshape(1, width)
-    return pl.pallas_call(
-        toeplitz_kernel,
-        out_shape=(
-            jax.ShapeDtypeStruct((LANES, width), jnp.bfloat16),
-            jax.ShapeDtypeStruct((2 * LANES, width), jnp.bfloat16),
-        ),
-    )(taps)
-
-
 def main_kernel(
     n_chan, n_tm, lag_total, half, left,
-    raw_ref, high_ref, both_ref, out_ref,
-    low_halo, high_halo, win_high, win_low, wide, stack, blocks, part, near, sent, far,
-    halo_send, halo_recv, gather_send, gather_recv, near_send, near_recv, far_send, far_recv,
+    raw_ref, taps_ref, mask_ref, out_ref,
+    local, low_halo, high_halo, win_high, win_low, wide, stack, blocks, part, near, sent, far,
+    local_sem, halo_send, halo_recv, gather_send, gather_recv, near_send, near_recv, far_send, far_recv,
 ):
     chan, tm = lax.axis_index("chan"), lax.axis_index("tm")
     channels, seg = raw_ref.shape
@@ -47,6 +24,8 @@
     chip, core = tm // 2, lax.rem(tm, 2)
     lag_rows = channels * (lag_total // n_tm)
 
+    own_copy = pltpu.make_async_copy(raw_ref, local, local_sem)
+    own_copy.start()
     barrier = pltpu.get_barrier_semaphore()
     for d in range(1, n_tm):
         pl.semaphore_signal(
@@ -76,25 +55,37 @@
     )
     to_right.start()
     to_left.start()
+
+    width = 2 * half + LANES
+    taps = jnp.concatenate(
+        [taps_ref[...].reshape(1, 2 * half), jnp.zeros((1, LANES), jnp.float32)], axis=1
+    )
+    matrix = pltpu.roll(
+        jnp.broadcast_to(taps, (LANES, width)), 0, 1, stride=1, stride_axis=0
+    )
+    matrix_high = matrix.astype(jnp.bfloat16)
+    matrix_low = (matrix - matrix_high.astype(jnp.float32)).astype(jnp.bfloat16)
+    matrix_both = jnp.concatenate([matrix_high, matrix_low], axis=0)
+
+    own_copy.wait()
     to_right.wait_recv()
     to_left.wait_recv()
     not_first = (tm > 0).astype(jnp.float32)
     not_last = (tm < n_tm - 1).astype(jnp.float32)
     padded = jnp.concatenate(
-        [low_halo[...] * not_first, raw_ref[...], high_halo[...] * not_last], axis=1
+        [low_halo[...] * not_first, local[...], high_halo[...] * not_last], axis=1
     )
     high = padded.astype(jnp.bfloat16)
     low = (padded - high.astype(jnp.float32)).astype(jnp.bfloat16)
     pieces = (seg + left) // LANES
-    width = 2 * half + LANES
     for b in range(pieces):
         win_high[pl.ds(b * channels, channels)] = high[:, b * LANES : b * LANES + width]
         win_low[pl.ds(b * channels, channels)] = low[:, b * LANES : b * LANES + width]
     both = lax.dot_general(
-        win_high[...], both_ref[...], NT, preferred_element_type=jnp.float32
+        win_high[...], matrix_both, NT, preferred_element_type=jnp.float32
     )
     rest = lax.dot_general(
-        win_low[...], high_ref[...], NT, preferred_element_type=jnp.float32
+        win_low[...], matrix_high, NT, preferred_element_type=jnp.float32
     )
     total = both[:, :LANES] + (both[:, LANES:] + rest)
     rounded = total.astype(jnp.bfloat16)
@@ -172,7 +163,12 @@
     for d in range(chips - 1):
         far_copies[d].wait_recv()
         own = own + far[d].astype(jnp.float32)
-    out_ref[...] = own
+    place = lax.broadcasted_iota(jnp.int32, (1, n_chan * channels), 1)
+    weights = jnp.zeros((1, n_chan * channels), jnp.float32)
+    for j in range(n_chan):
+        inside = (place >= j * channels) & (place < (j + 1) * channels)
+        weights = jnp.where(inside, mask_ref[chan, j].astype(jnp.float32), weights)
+    out_ref[...] = own * (weights * float(seg * n_tm) ** (-0.5))
 
     to_right.wait_send()
     to_left.wait_send()
@@ -192,14 +188,18 @@
     every = n_chan * channels
     width = taps + LANES
     windows = channels * (seg + left) // LANES
-    high, both = toeplitz(whitening)
     dma = pltpu.SemaphoreType.DMA
     sums = pl.pallas_call(
         functools.partial(main_kernel, n_chan, n_tm, lag_total, half, left),
         out_shape=jax.ShapeDtypeStruct((rows, every), jnp.float32),
-        in_specs=[pl.BlockSpec(memory_space=pltpu.VMEM)] * 3,
+        in_specs=[
+            pl.BlockSpec(memory_space=pl.ANY),
+            pl.BlockSpec(memory_space=pltpu.VMEM),
+            pl.BlockSpec(memory_space=pltpu.SMEM),
+        ],
         out_specs=pl.BlockSpec(memory_space=pltpu.VMEM),
         scratch_shapes=[
+            pltpu.VMEM((channels, seg), jnp.float32),
             pltpu.VMEM((channels, half + left), jnp.float32),
             pltpu.VMEM((channels, half), jnp.float32),
             pltpu.VMEM((windows, width), jnp.bfloat16),
@@ -211,6 +211,7 @@
             pltpu.VMEM((chips, rows, every), jnp.float32),
             pltpu.VMEM((chips, rows, every), jnp.bfloat16),
             pltpu.VMEM((chips, rows, every), jnp.bfloat16),
+            dma,
             dma((2,)),
             dma((2,)),
             dma((n_chan,)),
@@ -221,13 +222,10 @@
             dma((chips,)),
         ],
         compiler_params=pltpu.CompilerParams(
-            collective_id=0, has_side_effects=True, vmem_limit_bytes=40 * 1024 * 1024
+            collective_id=0, has_side_effects=True, vmem_limit_bytes=58 * 1024 * 1024
         ),
-    )(raw_strain, high, both)
-    scaling = float(seg * n_tm) ** (-0.5)
-    mask_row = lax.dynamic_index_in_dim(block_mask, lax.axis_index("chan"), 0, keepdims=False)
-    weights = jnp.repeat(mask_row.astype(jnp.float32) * scaling, channels)
-    return old_stack + sums.reshape(lags, channels, every) * weights
+    )(raw_strain, whitening, block_mask)
+    return old_stack + sums.reshape(lags, channels, every)
 
 
 def solution(mesh):

time: 40.7 us -> 36.4 us (0.89)
  local copies, waits for them, and re-layouts: 4.42 us -> 0.01 us
    unnamed x8 -> x2, local copies, waits for them, and re-layouts: 2.98 us -> 0.01 us
    pallas_call x1 -> x0, Pallas kernels: 1.83 us -> none  [toeplitz(): pl.pallas_call(toeplitz_kernel, out_shape=(jax.ShapeDtypeStruct((LANES, w...]
    pallas_call x1, Pallas kernels: 32.7 us -> 34.4 us  [shards(): pl.pallas_call(functools.partial(main_kernel, n_chan, n_tm, lag_total, ha...]
    add x1, other arithmetic: 0.74 us -> 1.69 us  [shards(): return old_stack + sums.reshape(lags, channels, every)]
    mul x1 -> x0, other arithmetic: 0.69 us -> none  [shards(): weights = jnp.repeat(mask_row.astype(jnp.float32) * scaling, channels)]
    pad x1 -> x0, local copies, waits for them, and re-layouts: 0.69 us -> none  [toeplitz(): taps = jnp.pad(whitening, (0, LANES)).reshape(1, width)]
    reshape x1 -> x0, local copies, waits for them, and re-layouts: 0.6 us -> none  [toeplitz(): taps = jnp.pad(whitening, (0, LANES)).reshape(1, width)]
where the time goes in v2:
time: 36.4 us; the launch traced here: 36.1 us
  Pallas kernels  34.4 us (95%)
  other arithmetic  1.69 us (5%)
    pallas_call x1, Pallas kernels, shards(): pl.pallas_call(functools.partial(main_kernel, n_chan, n_tm, lag_total, ha...  34.4 us
    add x1, other arithmetic, shards(): return old_stack + sums.reshape(lags, channels, every)  1.69 us

profile of v2, /device:TPU:0, one launch (start us, length us, event | category | flops | bytes accessed | tf_op | source)
XLA Modules:
  0.0 36.1 jit_solution(6098412037831096152)
XLA Ops:
  0.0 0.0 copy-start
  0.0 34.4 %shard_map.46 = f32[256,256]{1,0:T(8,128)} custom-call(f32[64,1024]{1,0:T(8,128)} %raw_ref.1, f32[1024]{0:T(1024)} %taps_ref.1, s32[4,4]{1,0:T(4,128)} %mask_ref.1), custom_call_target="tpu_custom_call" | custom-call | tf_op jit(solution)/shard_map/pallas_call | solution.py:192
  34.4 0.0 copy-done
  34.4 1.7 %add.3 = f32[4,64,256]{2,1,0:T(8,128)} add(f32[4,64,256]{2,1,0:T(8,128)S(1)} %copy-done, f32[4,64,256]{2,1,0:T(8,128)} %bitcast.1) | non-fusion elementwise | flops 65536 | bytes 786432 | tf_op jit(solution)/shard_map/add | solution.py:228
Async XLA Ops:
  0.0 34.4 %copy-start = (f32[4,64,256]{2,1,0:T(8,128)S(1)}, f32[4,64,256]{2,1,0:T(8,128)}, u32[]{:S(2)}) copy-start(f32[4,64,256]{2,1,0:T(8,128)} %param.7) | copy-start | bytes 786436

commit v3 on v2

--- a/solution.py
+++ b/solution.py
@@ -15,7 +15,7 @@
 def main_kernel(
     n_chan, n_tm, lag_total, half, left,
     raw_ref, taps_ref, mask_ref, out_ref,
-    local, low_halo, high_halo, win_high, win_low, wide, stack, blocks, part, near, sent, far,
+    local, low_halo, high_halo, win_high, win_low, wide, stack, blocks, part, near, sent, far, mine,
     local_sem, halo_send, halo_recv, gather_send, gather_recv, near_send, near_recv, far_send, far_recv,
 ):
     chan, tm = lax.axis_index("chan"), lax.axis_index("tm")
@@ -95,19 +95,54 @@
             b * channels : (b + 1) * channels
         ]
 
-    gathers = []
-    for d in range(1, n_chan):
-        gathers.append(
-            pltpu.make_async_remote_copy(
-                src_ref=blocks.at[chan],
-                dst_ref=blocks.at[chan],
-                send_sem=gather_send.at[d],
-                recv_sem=gather_recv.at[d],
-                device_id=(lax.rem(chan + d, n_chan), tm),
+    last = n_chan - 1
+
+    def hop(step, way):
+        lane = 0 if way > 0 else 1
+
+        def copy(block):
+            return pltpu.make_async_remote_copy(
+                src_ref=blocks.at[block],
+                dst_ref=blocks.at[block],
+                send_sem=gather_send.at[lane, step],
+                recv_sem=gather_recv.at[lane, step],
+                device_id=(lax.rem(chan + way + n_chan, n_chan), tm),
                 device_id_type=MESH,
             )
-        )
-        gathers[-1].start()
+
+        if way > 0:
+            sends = (chan >= step) & (chan < last)
+            gets = chan >= step + 1
+        else:
+            sends = (chan <= last - step) & (chan > 0)
+            gets = chan <= last - 1 - step
+        return copy, sends, chan - way * step, gets, chan - way * (step + 1)
+
+    def start_hops(step):
+        for way in (1, -1):
+            copy, sends, block, _, _ = hop(step, way)
+
+            @pl.when(sends)
+            def _():
+                copy(block).start()
+
+    def finish_hops(step):
+        for way in (1, -1):
+            copy, _, _, gets, block = hop(step, way)
+
+            @pl.when(gets)
+            def _():
+                copy(block).wait_recv()
+
+    def sent_hops(step):
+        for way in (1, -1):
+            copy, sends, block, _, _ = hop(step, way)
+
+            @pl.when(sends)
+            def _():
+                copy(block).wait_send()
+
+    start_hops(0)
 
     exact = rounded.astype(jnp.float32)
     for b in range(pieces):
@@ -117,62 +152,96 @@
         q, row = divmod(lag * channels, lag_rows)
         moved = wide[...] if lag == 0 else pltpu.roll(wide[...], lag, 1)
         stack[q, pl.ds(row, channels)] = moved[:, left:].astype(jnp.bfloat16)
-    for copy in gathers:
-        copy.wait_recv()
-
-    partner = blocks[...].reshape(n_chan * channels, seg)
-
-    def partial_sums(q):
+    finish_hops(0)
+    if n_chan > 2:
+        start_hops(1)
+
+    rounds = n_chan // 2
+    span = 2 * channels
+    near_copies, far_copies = [], []
+
+    def pair_of(turn):
+        return lax.rem(chan // 2 + turn, rounds)
+
+    def partners(turn):
+        return blocks[pl.ds(2 * pair_of(turn), 2)].reshape(span, seg)
+
+    def partial_sums(q, partner):
         return lax.dot_general(stack[q], partner, NT, preferred_element_type=jnp.float32)
 
-    near_copies = []
-    for d in range(chips):
-        owner = lax.rem(chip + d + 1, chips)
-        part[d] = partial_sums(owner * 2 + 1 - core)
-        near_copies.append(
-            pltpu.make_async_remote_copy(
-                src_ref=part.at[d],
-                dst_ref=near.at[d],
-                send_sem=near_send.at[d],
-                recv_sem=near_recv.at[d],
-                device_id=(chan, chip * 2 + 1 - core),
-                device_id_type=MESH,
+    def send_near(turn):
+        partner = partners(turn)
+        for d in range(chips):
+            owner = lax.rem(chip + d + 1, chips)
+            slot = turn * chips + d
+            part[slot] = partial_sums(owner * 2 + 1 - core, partner)
+            near_copies.append(
+                pltpu.make_async_remote_copy(
+                    src_ref=part.at[slot],
+                    dst_ref=near.at[slot],
+                    send_sem=near_send.at[slot],
+                    recv_sem=near_recv.at[slot],
+                    device_id=(chan, chip * 2 + 1 - core),
+                    device_id_type=MESH,
+                )
             )
+            near_copies[-1].start()
+
+    def send_far(turn):
+        partner = partners(turn)
+        for d in range(chips):
+            owner = lax.rem(chip + d + 1, chips)
+            slot = turn * chips + d
+            own = partial_sums(owner * 2 + core, partner)
+            near_copies[slot].wait_recv()
+            if d == chips - 1:
+                return own + near[slot]
+            sent[slot] = (own + near[slot]).astype(jnp.bfloat16)
+            far_copies.append(
+                pltpu.make_async_remote_copy(
+                    src_ref=sent.at[slot],
+                    dst_ref=far.at[slot],
+                    send_sem=far_send.at[slot],
+                    recv_sem=far_recv.at[slot],
+                    device_id=(chan, owner * 2 + core),
+                    device_id_type=MESH,
+                )
+            )
+            far_copies[-1].start()
+
+    for turn in range(rounds):
+        send_near(turn)
+        if turn == 0 and n_chan > 2:
+            finish_hops(1)
+            if n_chan > 3:
+                start_hops(2)
+        mine[turn] = send_far(turn)
+        if turn == 0:
+            for step in range(2, n_chan - 1):
+                finish_hops(step)
+                if step + 1 < n_chan - 1:
+                    start_hops(step + 1)
+
+    for turn in range(rounds):
+        own = mine[turn]
+        for d in range(chips - 1):
+            far_copies[turn * (chips - 1) + d].wait_recv()
+            own = own + far[turn * chips + d].astype(jnp.float32)
+        pair = pair_of(turn)
+        place = lax.broadcasted_iota(jnp.int32, (1, span), 1)
+        weights = jnp.where(
+            place < channels,
+            mask_ref[chan, 2 * pair].astype(jnp.float32),
+            mask_ref[chan, 2 * pair + 1].astype(jnp.float32),
         )
-        near_copies[-1].start()
-    far_copies = []
-    for d in range(chips - 1):
-        owner = lax.rem(chip + d + 1, chips)
-        own = partial_sums(owner * 2 + core)
-        near_copies[d].wait_recv()
-        sent[d] = (own + near[d]).astype(jnp.bfloat16)
-        far_copies.append(
-            pltpu.make_async_remote_copy(
-                src_ref=sent.at[d],
-                dst_ref=far.at[d],
-                send_sem=far_send.at[d],
-                recv_sem=far_recv.at[d],
-                device_id=(chan, owner * 2 + core),
-                device_id_type=MESH,
-            )
-        )
-        far_copies[-1].start()
-    own = partial_sums(chip * 2 + core)
-    near_copies[chips - 1].wait_recv()
-    own = own + near[chips - 1]
-    for d in range(chips - 1):
-        far_copies[d].wait_recv()
-        own = own + far[d].astype(jnp.float32)
-    place = lax.broadcasted_iota(jnp.int32, (1, n_chan * channels), 1)
-    weights = jnp.zeros((1, n_chan * channels), jnp.float32)
-    for j in range(n_chan):
-        inside = (place >= j * channels) & (place < (j + 1) * channels)
-        weights = jnp.where(inside, mask_ref[chan, j].astype(jnp.float32), weights)
-    out_ref[...] = own * (weights * float(seg * n_tm) ** (-0.5))
+        columns = pl.ds(pl.multiple_of(pair * span, span), span)
+        out_ref[:, columns] = own * (weights * float(seg * n_tm) ** (-0.5))
 
     to_right.wait_send()
     to_left.wait_send()
-    for copy in gathers + near_copies + far_copies:
+    for step in range(n_chan - 1):
+        sent_hops(step)
+    for copy in near_copies + far_copies:
         copy.wait_send()
 
 
@@ -186,6 +255,8 @@
     chips = n_tm // 2
     rows = channels * lags
     every = n_chan * channels
+    span = 2 * channels
+    slots = chips * (n_chan // 2)
     width = taps + LANES
     windows = channels * (seg + left) // LANES
     dma = pltpu.SemaphoreType.DMA
@@ -207,19 +278,20 @@
             pltpu.VMEM((channels, seg + left), jnp.float32),
             pltpu.VMEM((n_tm, rows, seg), jnp.bfloat16),
             pltpu.VMEM((n_chan, channels, seg), jnp.bfloat16),
-            pltpu.VMEM((chips, rows, every), jnp.float32),
-            pltpu.VMEM((chips, rows, every), jnp.float32),
-            pltpu.VMEM((chips, rows, every), jnp.bfloat16),
-            pltpu.VMEM((chips, rows, every), jnp.bfloat16),
+            pltpu.VMEM((slots, rows, span), jnp.float32),
+            pltpu.VMEM((slots, rows, span), jnp.float32),
+            pltpu.VMEM((slots, rows, span), jnp.bfloat16),
+            pltpu.VMEM((slots, rows, span), jnp.bfloat16),
+            pltpu.VMEM((n_chan // 2, rows, span), jnp.float32),
             dma,
             dma((2,)),
             dma((2,)),
-            dma((n_chan,)),
-            dma((n_chan,)),
-            dma((chips,)),
-            dma((chips,)),
-            dma((chips,)),
-            dma((chips,)),
+            dma((2, n_chan)),
+            dma((2, n_chan)),
+            dma((slots,)),
+            dma((slots,)),
+            dma((slots,)),
+            dma((slots,)),
         ],
         compiler_params=pltpu.CompilerParams(
             collective_id=0, has_side_effects=True, vmem_limit_bytes=58 * 1024 * 1024

time: 36.4 us -> 36.2 us (level)
  no operation moved by 1% of the time
where the time goes in v3:
time: 36.2 us; the launch traced here: 36 us
  Pallas kernels  34.3 us (95%)
  other arithmetic  1.69 us (5%)
    pallas_call x1, Pallas kernels, shards(): pl.pallas_call(functools.partial(main_kernel, n_chan, n_tm, lag_total, ha...  34.3 us
    add x1, other arithmetic, shards(): return old_stack + sums.reshape(lags, channels, every)  1.69 us

profile of v3, /device:TPU:0, one launch (start us, length us, event | category | flops | bytes accessed | tf_op | source)
XLA Modules:
  0.0 36.0 jit_solution(10086431528737329338)
XLA Ops:
  0.0 0.0 copy-start
  0.0 34.3 %shard_map.46 = f32[256,256]{1,0:T(8,128)} custom-call(f32[64,1024]{1,0:T(8,128)} %raw_ref.1, f32[1024]{0:T(1024)} %taps_ref.1, s32[4,4]{1,0:T(4,128)} %mask_ref.1), custom_call_target="tpu_custom_call" | custom-call | tf_op jit(solution)/shard_map/pallas_call | solution.py:263
  34.3 0.0 copy-done
  34.3 1.7 %add.3 = f32[4,64,256]{2,1,0:T(8,128)} add(f32[4,64,256]{2,1,0:T(8,128)S(1)} %copy-done, f32[4,64,256]{2,1,0:T(8,128)} %bitcast.1) | non-fusion elementwise | flops 65536 | bytes 786432 | tf_op jit(solution)/shard_map/add | solution.py:300
Async XLA Ops:
  0.0 34.3 %copy-start = (f32[4,64,256]{2,1,0:T(8,128)S(1)}, f32[4,64,256]{2,1,0:T(8,128)}, u32[]{:S(2)}) copy-start(f32[4,64,256]{2,1,0:T(8,128)} %param.7) | copy-start | bytes 786436

commit v4 on v3

--- a/solution.py
+++ b/solution.py
@@ -26,6 +26,13 @@
 
     own_copy = pltpu.make_async_copy(raw_ref, local, local_sem)
     own_copy.start()
+    def other_chip(d):
+        offset, result, bit = chips - 1 - d, 0, 1
+        while bit < chips:
+            result = result + bit * lax.rem(chip // bit + offset // bit % 2, 2)
+            bit *= 2
+        return result
+
     barrier = pltpu.get_barrier_semaphore()
     for d in range(1, n_tm):
         pl.semaphore_signal(
@@ -97,15 +104,19 @@
 
     last = n_chan - 1
 
-    def hop(step, way):
+    pieces_of = 4 if channels % 64 == 0 else 1
+    depth = channels // pieces_of
+
+    def hop(step, way, piece):
+        rows = pl.ds(piece * depth, depth)
         lane = 0 if way > 0 else 1
 
         def copy(block):
             return pltpu.make_async_remote_copy(
-                src_ref=blocks.at[block],
-                dst_ref=blocks.at[block],
-                send_sem=gather_send.at[lane, step],
-                recv_sem=gather_recv.at[lane, step],
+                src_ref=blocks.at[block, rows],
+                dst_ref=blocks.at[block, rows],
+                send_sem=gather_send.at[lane, step, piece],
+                recv_sem=gather_recv.at[lane, step, piece],
                 device_id=(lax.rem(chan + way + n_chan, n_chan), tm),
                 device_id_type=MESH,
             )
@@ -118,31 +129,38 @@
             gets = chan <= last - 1 - step
         return copy, sends, chan - way * step, gets, chan - way * (step + 1)
 
-    def start_hops(step):
+    def start_hops(step, piece):
         for way in (1, -1):
-            copy, sends, block, _, _ = hop(step, way)
+            copy, sends, block, _, _ = hop(step, way, piece)
 
             @pl.when(sends)
             def _():
                 copy(block).start()
 
-    def finish_hops(step):
+    def finish_hops(step, piece):
         for way in (1, -1):
-            copy, _, _, gets, block = hop(step, way)
+            copy, _, _, gets, block = hop(step, way, piece)
 
             @pl.when(gets)
             def _():
                 copy(block).wait_recv()
 
-    def sent_hops(step):
+    def sent_hops(step, piece):
         for way in (1, -1):
-            copy, sends, block, _, _ = hop(step, way)
+            copy, sends, block, _, _ = hop(step, way, piece)
 
             @pl.when(sends)
             def _():
                 copy(block).wait_send()
 
-    start_hops(0)
+    def hand_on(step):
+        for piece in range(pieces_of):
+            finish_hops(step, piece)
+            if step + 1 < n_chan - 1:
+                start_hops(step + 1, piece)
+
+    for piece in range(pieces_of):
+        start_hops(0, piece)
 
     exact = rounded.astype(jnp.float32)
     for b in range(pieces):
@@ -152,9 +170,7 @@
         q, row = divmod(lag * channels, lag_rows)
         moved = wide[...] if lag == 0 else pltpu.roll(wide[...], lag, 1)
         stack[q, pl.ds(row, channels)] = moved[:, left:].astype(jnp.bfloat16)
-    finish_hops(0)
-    if n_chan > 2:
-        start_hops(1)
+    hand_on(0)
 
     rounds = n_chan // 2
     span = 2 * channels
@@ -172,7 +188,7 @@
     def send_near(turn):
         partner = partners(turn)
         for d in range(chips):
-            owner = lax.rem(chip + d + 1, chips)
+            owner = other_chip(d)
             slot = turn * chips + d
             part[slot] = partial_sums(owner * 2 + 1 - core, partner)
             near_copies.append(
@@ -190,7 +206,7 @@
     def send_far(turn):
         partner = partners(turn)
         for d in range(chips):
-            owner = lax.rem(chip + d + 1, chips)
+            owner = other_chip(d)
             slot = turn * chips + d
             own = partial_sums(owner * 2 + core, partner)
             near_copies[slot].wait_recv()
@@ -212,15 +228,11 @@
     for turn in range(rounds):
         send_near(turn)
         if turn == 0 and n_chan > 2:
-            finish_hops(1)
-            if n_chan > 3:
-                start_hops(2)
+            hand_on(1)
         mine[turn] = send_far(turn)
         if turn == 0:
             for step in range(2, n_chan - 1):
-                finish_hops(step)
-                if step + 1 < n_chan - 1:
-                    start_hops(step + 1)
+                hand_on(step)
 
     for turn in range(rounds):
         own = mine[turn]
@@ -240,7 +252,8 @@
     to_right.wait_send()
     to_left.wait_send()
     for step in range(n_chan - 1):
-        sent_hops(step)
+        for piece in range(pieces_of):
+            sent_hops(step, piece)
     for copy in near_copies + far_copies:
         copy.wait_send()
 
@@ -286,8 +299,8 @@
             dma,
             dma((2,)),
             dma((2,)),
-            dma((2, n_chan)),
-            dma((2, n_chan)),
+            dma((2, n_chan, 4)),
+            dma((2, n_chan, 4)),
             dma((slots,)),
             dma((slots,)),
             dma((slots,)),

time: 36.2 us -> 34.1 us (0.942)
  Pallas kernels: 34.3 us -> 32.3 us
    pallas_call x1, Pallas kernels: 34.3 us -> 32.3 us  [shards(): pl.pallas_call(functools.partial(main_kernel, n_chan, n_tm, lag_total, ha...]
where the time goes in v4:
time: 34.1 us; the launch traced here: 34 us
  Pallas kernels  32.3 us (95%)
  other arithmetic  1.69 us (5%)
    pallas_call x1, Pallas kernels, shards(): pl.pallas_call(functools.partial(main_kernel, n_chan, n_tm, lag_total, ha...  32.3 us
    add x1, other arithmetic, shards(): return old_stack + sums.reshape(lags, channels, every)  1.69 us

profile of v4, /device:TPU:0, one launch (start us, length us, event | category | flops | bytes accessed | tf_op | source)
XLA Modules:
  0.0 34.0 jit_solution(17633053222054867697)
XLA Ops:
  0.0 0.0 copy-start
  0.0 32.3 %shard_map.46 = f32[256,256]{1,0:T(8,128)} custom-call(f32[64,1024]{1,0:T(8,128)} %raw_ref.1, f32[1024]{0:T(1024)} %taps_ref.1, s32[4,4]{1,0:T(4,128)} %mask_ref.1), custom_call_target="tpu_custom_call" | custom-call | tf_op jit(solution)/shard_map/pallas_call | solution.py:276
  32.3 0.0 copy-done
  32.3 1.7 %add.3 = f32[4,64,256]{2,1,0:T(8,128)} add(f32[4,64,256]{2,1,0:T(8,128)S(1)} %copy-done, f32[4,64,256]{2,1,0:T(8,128)} %bitcast.1) | non-fusion elementwise | flops 65536 | bytes 786432 | tf_op jit(solution)/shard_map/add | solution.py:313
Async XLA Ops:
  0.0 32.3 %copy-start = (f32[4,64,256]{2,1,0:T(8,128)S(1)}, f32[4,64,256]{2,1,0:T(8,128)}, u32[]{:S(2)}) copy-start(f32[4,64,256]{2,1,0:T(8,128)} %param.7) | copy-start | bytes 786436

commit v5 on v4

--- a/solution.py
+++ b/solution.py
@@ -34,15 +34,22 @@
         return result
 
     barrier = pltpu.get_barrier_semaphore()
-    for d in range(1, n_tm):
-        pl.semaphore_signal(
-            barrier, inc=1, device_id=(chan, lax.rem(tm + d, n_tm)), device_id_type=MESH
-        )
-    for d in range(1, n_chan):
-        pl.semaphore_signal(
-            barrier, inc=1, device_id=(lax.rem(chan + d, n_chan), tm), device_id_type=MESH
-        )
-    pl.semaphore_wait(barrier, n_tm - 1 + n_chan - 1)
+    last = n_chan - 1
+    others = [lax.rem(tm + 1, n_tm), lax.rem(tm + n_tm - 1, n_tm)]
+    others += [other_chip(d) * 2 + core for d in range(chips - 1)]
+    for other in others:
+        pl.semaphore_signal(barrier, inc=1, device_id=(chan, other), device_id_type=MESH)
+
+    @pl.when(chan > 0)
+    def _():
+        pl.semaphore_signal(barrier, inc=1, device_id=(chan - 1, tm), device_id_type=MESH)
+
+    @pl.when(chan < last)
+    def _():
+        pl.semaphore_signal(barrier, inc=1, device_id=(chan + 1, tm), device_id_type=MESH)
+
+    beside = (chan > 0).astype(jnp.int32) + (chan < last).astype(jnp.int32)
+    pl.semaphore_wait(barrier, len(others) + beside)
 
     to_right = pltpu.make_async_remote_copy(
         src_ref=raw_ref.at[:, pl.ds(seg - half - left, half + left)],
@@ -60,8 +67,13 @@
         device_id=(chan, lax.rem(tm + n_tm - 1, n_tm)),
         device_id_type=MESH,
     )
-    to_right.start()
-    to_left.start()
+    @pl.when(tm < n_tm - 1)
+    def _():
+        to_right.start()
+
+    @pl.when(tm > 0)
+    def _():
+        to_left.start()
 
     width = 2 * half + LANES
     taps = jnp.concatenate(
@@ -75,12 +87,26 @@
     matrix_both = jnp.concatenate([matrix_high, matrix_low], axis=0)
 
     own_copy.wait()
-    to_right.wait_recv()
-    to_left.wait_recv()
+
+    @pl.when(tm > 0)
+    def _():
+        to_right.wait_recv()
+
+    @pl.when(tm == 0)
+    def _():
+        low_halo[...] = jnp.zeros_like(low_halo)
+
+    @pl.when(tm < n_tm - 1)
+    def _():
+        to_left.wait_recv()
+
+    @pl.when(tm == n_tm - 1)
+    def _():
+        high_halo[...] = jnp.zeros_like(high_halo)
+
     not_first = (tm > 0).astype(jnp.float32)
-    not_last = (tm < n_tm - 1).astype(jnp.float32)
     padded = jnp.concatenate(
-        [low_halo[...] * not_first, local[...], high_halo[...] * not_last], axis=1
+        [low_halo[...], local[...], high_halo[...]], axis=1
     )
     high = padded.astype(jnp.bfloat16)
     low = (padded - high.astype(jnp.float32)).astype(jnp.bfloat16)
@@ -153,11 +179,14 @@
             def _():
                 copy(block).wait_send()
 
+    def hand_on_piece(step, piece):
+        finish_hops(step, piece)
+        if step + 1 < n_chan - 1:
+            start_hops(step + 1, piece)
+
     def hand_on(step):
         for piece in range(pieces_of):
-            finish_hops(step, piece)
-            if step + 1 < n_chan - 1:
-                start_hops(step + 1, piece)
+            hand_on_piece(step, piece)
 
     for piece in range(pieces_of):
         start_hops(0, piece)
@@ -170,7 +199,8 @@
         q, row = divmod(lag * channels, lag_rows)
         moved = wide[...] if lag == 0 else pltpu.roll(wide[...], lag, 1)
         stack[q, pl.ds(row, channels)] = moved[:, left:].astype(jnp.bfloat16)
-    hand_on(0)
+        if (lag + 1) * pieces_of % lag_total == 0:
+            hand_on_piece(0, (lag + 1) * pieces_of // lag_total - 1)
 
     rounds = n_chan // 2
     span = 2 * channels
@@ -249,8 +279,14 @@
         columns = pl.ds(pl.multiple_of(pair * span, span), span)
         out_ref[:, columns] = own * (weights * float(seg * n_tm) ** (-0.5))
 
-    to_right.wait_send()
-    to_left.wait_send()
+    @pl.when(tm < n_tm - 1)
+    def _():
+        to_right.wait_send()
+
+    @pl.when(tm > 0)
+    def _():
+        to_left.wait_send()
+
     for step in range(n_chan - 1):
         for piece in range(pieces_of):
             sent_hops(step, piece)

time: 34.1 us -> 32.8 us (0.962)
  Pallas kernels: 32.3 us -> 30.9 us
    pallas_call x1, Pallas kernels: 32.3 us -> 30.9 us  [shards(): pl.pallas_call(functools.partial(main_kernel, n_chan, n_tm, lag_total, ha...]
where the time goes in v5:
time: 32.8 us; the launch traced here: 32.6 us
  Pallas kernels  30.9 us (94%)
  other arithmetic  1.69 us (5%)
    pallas_call x1, Pallas kernels, shards(): pl.pallas_call(functools.partial(main_kernel, n_chan, n_tm, lag_total, ha...  30.9 us
    add x1, other arithmetic, shards(): return old_stack + sums.reshape(lags, channels, every)  1.69 us

profile of v5, /device:TPU:0, one launch (start us, length us, event | category | flops | bytes accessed | tf_op | source)
XLA Modules:
  0.0 32.6 jit_solution(14621774665767274815)
XLA Ops:
  0.0 0.0 copy-start
  0.0 30.9 %shard_map.46 = f32[256,256]{1,0:T(8,128)} custom-call(f32[64,1024]{1,0:T(8,128)} %raw_ref.1, f32[1024]{0:T(1024)} %taps_ref.1, s32[4,4]{1,0:T(4,128)} %mask_ref.1), custom_call_target="tpu_custom_call" | custom-call | tf_op jit(solution)/shard_map/pallas_call | solution.py:312
  30.9 0.0 copy-done
  30.9 1.7 %add.3 = f32[4,64,256]{2,1,0:T(8,128)} add(f32[4,64,256]{2,1,0:T(8,128)S(1)} %copy-done, f32[4,64,256]{2,1,0:T(8,128)} %bitcast.1) | non-fusion elementwise | flops 65536 | bytes 786432 | tf_op jit(solution)/shard_map/add | solution.py:349
Async XLA Ops:
  0.0 30.9 %copy-start = (f32[4,64,256]{2,1,0:T(8,128)S(1)}, f32[4,64,256]{2,1,0:T(8,128)}, u32[]{:S(2)}) copy-start(f32[4,64,256]{2,1,0:T(8,128)} %param.7) | copy-start | bytes 786436
